TPU v7x, 32 devices: a whole 2x2x4 slice. The times are simulated.
32 devices in a mesh: agg: 4 (over y, core), blk: 8 (over z, x).
Axes of the slice: x: 2, y: 2, z: 4, core: 2. Of those that a mesh axis runs over, the one named last changes fastest.
Arguments:
- right_side: float32 [128, 256, 128], P('blk', 'agg'), may hold values from -8 to 8
- coefficient: float32 [128, 256, 128], P('blk', 'agg'), may hold values from 0.05 to 2
Outputs:
- pressure: float32 [128, 256, 128], P('blk', 'agg')
All inputs are finite; a program needn't handle non-finite values.
Results may differ from a plain program's by a relative error of at most 0.0001.
Values sent between devices are 32-bit elements; how exact they have to be, the bound alone decides.
A program may use at most 128 MiB of HBM per device.

v0:
```python
import jax
import jax.numpy as jnp
from jax import lax
from jax.sharding import PartitionSpec as P

OMEGA = 0.8


def padded_2(x, sides, width):
    for axis, dim in sides:
        size, length = (lax.axis_size(axis), x.shape[dim])
        up = [(i, (i + 1) % size) for i in range(size - 1)]
        down = [(j, i) for i, j in up]
        last = lax.slice_in_dim(x, length - width, length, axis=dim)
        first = lax.slice_in_dim(x, 0, width, axis=dim)
        before = lax.ppermute(last, axis, up)
        after = lax.ppermute(first, axis, down)
        x = jnp.concatenate([before, x, after], axis=dim)
    return x


def from_partner(block, axis, apart):
    count = lax.axis_size(axis)
    route = []
    for low in range(count):
        high = low | 1 << apart
        if high != low and high < count:
            route += [(low, high), (high, low)]
    return lax.ppermute(block, axis, route)


def depth_pair(field):
    depth = field.shape[2]
    column = lax.broadcasted_iota(jnp.int32, field.shape, 2)
    ahead = jnp.where(column < depth - 1, jnp.roll(field, -1, axis=2), 0.0)
    behind = jnp.where(column > 0, jnp.roll(field, 1, axis=2), 0.0)
    return ahead + behind


def fine_apply(field, coef):
    padded = padded_2(field, (("blk", 0), ("agg", 1)), 1)
    total = padded[2:, 1:-1] + padded[:-2, 1:-1]
    total = total + padded[1:-1, 2:] + padded[1:-1, :-2]
    total = total + depth_pair(field)
    return (6.0 + coef) * field - total


def coarse_apply(field, coef, window):
    nx, ny, nz = field.shape
    padded = padded_2(field, (("blk", 0),), 1)
    total = padded[2:] + padded[:-2] + depth_pair(field)
    shaped = field.reshape(nx, ny // window, window, nz)
    edged = jnp.pad(shaped, ((0, 0), (0, 0), (1, 1), (0, 0)))
    total = total + (edged[:, :, 2:] + edged[:, :, :-2]).reshape(nx, ny, nz)
    return (6.0 + coef) * field - total


def restrict(field):
    nx, ny, nz = field.shape
    return field.reshape(nx // 2, 2, ny // 2, 2, nz // 2, 2).sum(axis=(1, 3, 5)) * 0.5


def prolong(field):
    nx, ny, nz = field.shape
    spread = jnp.broadcast_to(field[:, None, :, None, :, None], (nx, 2, ny, 2, nz, 2))
    return spread.reshape(2 * nx, 2 * ny, 2 * nz)


def joined(mine, other, upper):
    first = jnp.where(upper, other, mine)
    second = jnp.where(upper, mine, other)
    return jnp.concatenate((first, second), axis=1)


def shards(right_side, coefficient):
    levels = lax.axis_size("agg").bit_length() - 1
    rows = right_side.shape[1]
    place = lax.axis_index("agg")
    fine_inverse = 1.0 / (6.0 + coefficient)
    fine = OMEGA * right_side * fine_inverse
    fine = fine + OMEGA * (right_side - fine_apply(fine, coefficient)) * fine_inverse
    resid = right_side - fine_apply(fine, coefficient)
    level_rhs = restrict(resid)
    level_coef = coefficient
    rhs_list = []
    coef_list = []
    err_list = []
    for level in range(1, levels + 1):
        upper = place >> level - 1 & 1 == 1
        if level > 1:
            level_rhs = restrict(resid)
        level_coef = restrict(coefficient) if level == 1 else restrict(coef_list[-1])
        other_rhs, other_coef = from_partner((level_rhs, level_coef), "agg", level - 1)
        level_rhs = joined(level_rhs, other_rhs, upper)
        level_coef = joined(level_coef, other_coef, upper)
        inverse = 1.0 / (6.0 + level_coef)
        err = OMEGA * level_rhs * inverse
        if level == levels:
            err = err + OMEGA * (level_rhs - coarse_apply(err, level_coef, rows)) * inverse
        else:
            resid = level_rhs - coarse_apply(err, level_coef, rows)
        rhs_list.append(level_rhs)
        coef_list.append(level_coef)
        err_list.append(err)
    for level in range(levels, 0, -1):
        coarse = err_list[level - 1]
        high = place >> level - 1 & 1
        half = coarse.shape[1] // 2
        coarse = lax.dynamic_slice_in_dim(coarse, high * half, half, 1)
        if level > 1:
            below_rhs = rhs_list[level - 2]
            below_coef = coef_list[level - 2]
            merged = err_list[level - 2] + prolong(coarse)
            merged = merged + OMEGA * (below_rhs - coarse_apply(merged, below_coef, rows)) / (
                6.0 + below_coef
            )
            err_list[level - 2] = merged
        else:
            fine = fine + prolong(coarse)
            fine = fine + OMEGA * (right_side - fine_apply(fine, coefficient)) * fine_inverse
    return fine


def solution(mesh):
    placed = (P("blk", "agg", None), P("blk", "agg", None))
    return jax.shard_map(
        shards, mesh=mesh, in_specs=placed, out_specs=P("blk", "agg", None), check_vma=False
    )
```

profile of v0, /device:TPU:28, one launch (start us, length us, event | category | flops | bytes accessed | tf_op | source)
XLA Modules:
  0.0 274.3 jit_solution(5407644837371855523)
XLA Ops:
  1.3 3.3 %collective-permute-start = (f32[1,64,128]{2,1,0:T(8,128)S(1)}, f32[1,64,128]{2,1,0:T(8,128)S(1)}, u32[]{:S(2)}, u32[]{:S(2)}) collective-permute-start(f32[1,64,128]{2,1,0:T(8,128)S(1)} %get-tuple-element.28), channel_id=1, source_target_pairs={{1,0},{2,1},{3,2},{4,3},{5,4},{6,5},{7,6},{9,8},{10,9},{11,10},{12... | collective-permute-start | bytes 98312 | tf_op jit(solution)/shard_map/ppermute | solution.py:17
  7.3 35.6 %reshape.189 = f32[8,2,32,2,64,2]{5,4,3,2,1,0:T(8,128)} reshape(f32[16,64,128]{2,1,0:T(8,128)} %param.3) | data formatting | bytes 1048576 | tf_op jit(solution)/shard_map/reshape | solution.py:60
  42.9 12.2 %reduce_sum.37 = f32[8,32,64]{2,1,0:T(8,128)S(1)} reduce(f32[8,2,32,2,64,2]{5,4,3,2,1,0:T(8,128)} %reshape.189, f32[]{:T(128)} %constant.17.clone.1), dimensions={1,3,5}, to_apply=%region_1.2 | reduce | flops 114688 | bytes 589828 | tf_op jit(solution)/shard_map/reduce_sum | solution.py:60
  66.4 4.2 %collective-permute-start.4 = (f32[1,64,128]{2,1,0:T(8,128)S(1)}, f32[1,64,128]{2,1,0:T(8,128)S(1)}, u32[]{:S(2)}, u32[]{:S(2)}) collective-permute-start(f32[1,64,128]{2,1,0:T(8,128)S(1)} %get-tuple-element.22), channel_id=1, source_target_pairs={{1,0},{2,1},{3,2},{4,3},{5,4},{6,5},{7,6},{9,8},{10,9},{11,10},{12... | collective-permute-start | bytes 98312 | tf_op jit(solution)/shard_map/ppermute | solution.py:17
  72.8 4.6 %collective-permute-done.5 = f32[1,64,128]{2,1,0:T(8,128)S(1)} collective-permute-done((f32[1,64,128]{2,1,0:T(8,128)S(1)}, f32[1,64,128]{2,1,0:T(8,128)S(1)}, u32[]{:S(2)}, u32[]{:S(2)}) %collective-permute-start.5) | collective-permute-done | bytes 32800 | tf_op jit(solution)/shard_map/ppermute | solution.py:16
  84.8 34.9 %reshape.188 = f32[8,2,32,2,64,2]{5,4,3,2,1,0:T(8,128)} reshape(f32[16,64,128]{2,1,0:T(8,128)S(1)} %fusion.12) | data formatting | bytes 1048576 | tf_op jit(solution)/shard_map/reshape | solution.py:60
  119.6 12.2 %reduce_sum.36 = f32[8,32,64]{2,1,0:T(8,128)S(1)} reduce(f32[8,2,32,2,64,2]{5,4,3,2,1,0:T(8,128)} %reshape.188, f32[]{:T(128)} %constant.17.clone.1), dimensions={1,3,5}, to_apply=%region_0.1 | reduce | flops 114688 | bytes 589828 | tf_op jit(solution)/shard_map/reduce_sum | solution.py:60
  134.4 10.1 %reshape.192 = f32[4,2,32,2,32,2]{5,4,3,2,1,0:T(8,128)} reshape(f32[8,64,64]{2,1,0:T(8,128)S(1)} %get-tuple-element.37) | data formatting | bytes 262144 | tf_op jit(solution)/shard_map/reshape | solution.py:60
  144.5 4.1 %reduce_sum.39 = f32[4,32,32]{2,1,0:T(8,128)S(1)} reduce(f32[4,2,32,2,32,2]{5,4,3,2,1,0:T(8,128)} %reshape.192, f32[]{:T(128)} %constant.17.clone.1), dimensions={1,3,5}, to_apply=%region_3.4 | reduce | flops 28672 | bytes 147460 | tf_op jit(solution)/shard_map/reduce_sum | solution.py:60
  150.6 3.9 %collective-permute-start.11 = (f32[1,64,64]{2,1,0:T(8,128)S(1)}, f32[1,64,64]{2,1,0:T(8,128)S(1)}, u32[]{:S(2)}, u32[]{:S(2)}) collective-permute-start(f32[1,64,64]{2,1,0:T(8,128)S(1)} %get-tuple-element.44), channel_id=1, source_target_pairs={{0,1},{1,2},{2,3},{3,4},{4,5},{5,6},{6,7},{8,9},{9,10},{10,11},{11... | collective-permute-start | bytes 49160 | tf_op jit(solution)/shard_map/ppermute | solution.py:16
  159.3 10.1 %reshape.191 = f32[4,2,32,2,32,2]{5,4,3,2,1,0:T(8,128)} reshape(f32[8,64,64]{2,1,0:T(8,128)S(1)} %get-tuple-element.30) | data formatting | bytes 262144 | tf_op jit(solution)/shard_map/reshape | solution.py:60
  169.3 4.1 %reduce_sum.38 = f32[4,32,32]{2,1,0:T(8,128)S(1)} reduce(f32[4,2,32,2,32,2]{5,4,3,2,1,0:T(8,128)} %reshape.191, f32[]{:T(128)} %constant.17.clone.1), dimensions={1,3,5}, to_apply=%region_2.3 | reduce | flops 28672 | bytes 147460 | tf_op jit(solution)/shard_map/reduce_sum | solution.py:60
  178.0 2.9 %collective-permute-start.14 = (f32[1,64,32]{2,1,0:T(8,128)S(1)}, f32[1,64,32]{2,1,0:T(8,128)S(1)}, u32[]{:S(2)}, u32[]{:S(2)}) collective-permute-start(f32[1,64,32]{2,1,0:T(8,128)S(1)} %get-tuple-element.56), channel_id=1, source_target_pairs={{1,0},{2,1},{3,2},{4,3},{5,4},{6,5},{7,6},{9,8},{10,9},{11,10},{12... | collective-permute-start | bytes 24584 | tf_op jit(solution)/shard_map/ppermute | solution.py:17
  180.9 3.1 %collective-permute-start.15 = (f32[1,64,32]{2,1,0:T(8,128)S(1)}, f32[1,64,32]{2,1,0:T(8,128)S(1)}, u32[]{:S(2)}, u32[]{:S(2)}) collective-permute-start(f32[1,64,32]{2,1,0:T(8,128)S(1)} %get-tuple-element.57), channel_id=1, source_target_pairs={{0,1},{1,2},{2,3},{3,4},{4,5},{5,6},{6,7},{8,9},{9,10},{10,11},{11... | collective-permute-start | bytes 24584 | tf_op jit(solution)/shard_map/ppermute | solution.py:16
  184.2 3.5 %collective-permute-done.15 = f32[1,64,32]{2,1,0:T(8,128)S(1)} collective-permute-done((f32[1,64,32]{2,1,0:T(8,128)S(1)}, f32[1,64,32]{2,1,0:T(8,128)S(1)}, u32[]{:S(2)}, u32[]{:S(2)}) %collective-permute-start.15) | collective-permute-done | bytes 8224 | tf_op jit(solution)/shard_map/ppermute | solution.py:16
  188.5 3.9 %broadcast_in_dim.36 = f32[4,2,32,2,32,2]{5,4,3,2,1,0:T(8,128)} broadcast(f32[4,32,32]{2,1,0:T(8,128)S(1)} %fusion.61), dimensions={0,2,4} | broadcast | bytes 147456 | tf_op jit(solution)/shard_map/broadcast_in_dim | solution.py:65
  192.4 8.2 %reshape.194 = f32[8,64,64]{2,1,0:T(8,128)S(1)} reshape(f32[4,2,32,2,32,2]{5,4,3,2,1,0:T(8,128)} %broadcast_in_dim.36) | data formatting | bytes 262144 | tf_op jit(solution)/shard_map/reshape | solution.py:66
  201.6 8.2 %reshape.195 = f32[8,1,64,64]{3,2,0,1:T(8,128)S(1)} reshape(f32[4,2,32,2,32,2]{5,4,3,2,1,0:T(8,128)} %broadcast_in_dim.36) | data formatting | bytes 262144 | tf_op jit(solution)/shard_map/reshape | solution.py:66
  211.7 3.9 %collective-permute-start.17 = (f32[1,64,64]{2,1,0:T(8,128)S(1)}, f32[1,64,64]{2,1,0:T(8,128)S(1)}, u32[]{:S(2)}, u32[]{:S(2)}) collective-permute-start(f32[1,64,64]{2,1,0:T(8,128)S(1)} %get-tuple-element.36), channel_id=1, source_target_pairs={{0,1},{1,2},{2,3},{3,4},{4,5},{5,6},{6,7},{8,9},{9,10},{10,11},{11... | collective-permute-start | bytes 49160 | tf_op jit(solution)/shard_map/ppermute | solution.py:16
  220.6 11.4 %broadcast_in_dim.37 = f32[8,2,32,2,64,2]{5,4,3,2,1,0:T(8,128)} broadcast(f32[8,32,64]{2,1,0:T(8,128)S(1)} %fusion.50), dimensions={0,2,4} | broadcast | bytes 589824 | tf_op jit(solution)/shard_map/broadcast_in_dim | solution.py:65
  232.0 24.0 %reshape.197 = f32[16,64,128]{2,1,0:T(8,128)S(1)} reshape(f32[8,2,32,2,64,2]{5,4,3,2,1,0:T(8,128)} %broadcast_in_dim.37) | data formatting | bytes 1048576 | tf_op jit(solution)/shard_map/reshape | solution.py:66
  256.1 2.9 %collective-permute-start.18 = (f32[1,64,128]{2,1,0:T(8,128)S(1)}, f32[1,64,128]{2,1,0:T(8,128)S(1)}, u32[]{:S(2)}, u32[]{:S(2)}) collective-permute-start(f32[1,64,128]{2,1,0:T(8,128)S(1)} %get-tuple-element.16), channel_id=1, source_target_pairs={{1,0},{2,1},{3,2},{4,3},{5,4},{6,5},{7,6},{9,8},{10,9},{11,10},{12... | collective-permute-start | bytes 98312 | tf_op jit(solution)/shard_map/ppermute | solution.py:17
  259.0 2.9 %collective-permute-start.19 = (f32[1,64,128]{2,1,0:T(8,128)S(1)}, f32[1,64,128]{2,1,0:T(8,128)S(1)}, u32[]{:S(2)}, u32[]{:S(2)}) collective-permute-start(f32[1,64,128]{2,1,0:T(8,128)S(1)} %get-tuple-element.15), channel_id=1, source_target_pairs={{0,1},{1,2},{2,3},{3,4},{4,5},{5,6},{6,7},{8,9},{9,10},{10,11},{11... | collective-permute-start | bytes 98312 | tf_op jit(solution)/shard_map/ppermute | solution.py:16
  262.2 3.5 %collective-permute-done.19 = f32[1,64,128]{2,1,0:T(8,128)S(1)} collective-permute-done((f32[1,64,128]{2,1,0:T(8,128)S(1)}, f32[1,64,128]{2,1,0:T(8,128)S(1)}, u32[]{:S(2)}, u32[]{:S(2)}) %collective-permute-start.19) | collective-permute-done | bytes 32800 | tf_op jit(solution)/shard_map/ppermute | solution.py:16
  (87 shorter events, 56.3 us)
Async XLA Ops:
  1.3 55.9 %collective-permute-start = (f32[1,64,128]{2,1,0:T(8,128)S(1)}, f32[1,64,128]{2,1,0:T(8,128)S(1)}, u32[]{:S(2)}, u32[]{:S(2)}) collective-permute-start(f32[1,64,128]{2,1,0:T(8,128)S(1)} %get-tuple-element.28), channel_id=1, source_target_pairs={{1,0},{2,1},{3,2},{4,3},{5,4},{6,5},{7,6},{9,8},{10,9},{11,10},{12... | collective-permute-start | bytes 98312 | tf_op jit(solution)/shard_map/ppermute | solution.py:17
  4.6 60.1 %copy-start = (f32[16,64,128]{2,1,0:T(8,128)S(1)}, f32[16,64,128]{2,1,0:T(8,128)}, u32[]{:S(2)}) copy-start(f32[16,64,128]{2,1,0:T(8,128)} %param.3) | copy-start | bytes 1572868
  4.6 60.1 %copy-start.1 = (f32[16,64,128]{2,1,0:T(8,128)S(1)}, f32[16,64,128]{2,1,0:T(8,128)}, u32[]{:S(2)}) copy-start(f32[16,64,128]{2,1,0:T(8,128)} %param.2) | copy-start | bytes 1572868
  4.6 52.5 %collective-permute-start.1 = (f32[1,64,128]{2,1,0:T(8,128)S(1)}, f32[1,64,128]{2,1,0:T(8,128)S(1)}, u32[]{:S(2)}, u32[]{:S(2)}) collective-permute-start(f32[1,64,128]{2,1,0:T(8,128)S(1)} %get-tuple-element.27), channel_id=1, source_target_pairs={{0,1},{1,2},{2,3},{3,4},{4,5},{5,6},{6,7},{8,9},{9,10},{10,11},{11... | collective-permute-start | bytes 98312 | tf_op jit(solution)/shard_map/ppermute | solution.py:16
  55.8 76.1 %collective-permute-start.9 = (f32[8,32,64]{2,1,0:T(8,128)}, f32[8,32,64]{2,1,0:T(8,128)S(1)}, u32[]{:S(2)}, u32[]{:S(2)}) collective-permute-start(f32[8,32,64]{2,1,0:T(8,128)} %broadcast_multiply_fusion), channel_id=1, source_target_pairs={{0,8},{8,0},{16,24},{24,16},{1,9},{9,1},{17,25},{25,17},{2,10},{10... | collective-permute-start | bytes 196616 | tf_op jit(solution)/shard_map/ppermute | solution.py:29
  57.2 5.0 %collective-permute-start.2 = (f32[18,1,128]{2,1,0:T(1,128)S(1)}, f32[18,1,128]{2,1,0:T(1,128)S(1)}, u32[]{:S(2)}, u32[]{:S(2)}) collective-permute-start(f32[18,1,128]{2,1,0:T(1,128)S(1)} %get-tuple-element.9), channel_id=1, source_target_pairs={{8,0},{16,8},{24,16},{9,1},{17,9},{25,17},{10,2},{18,10},{26,18},{... | collective-permute-start | bytes 27656 | tf_op jit(solution)/shard_map/ppermute | solution.py:17
  59.7 5.0 %collective-permute-start.3 = (f32[18,1,128]{2,1,0:T(1,128)S(1)}, f32[18,1,128]{2,1,0:T(1,128)S(1)}, u32[]{:S(2)}, u32[]{:S(2)}) collective-permute-start(f32[18,1,128]{2,1,0:T(1,128)S(1)} %get-tuple-element.10), channel_id=1, source_target_pairs={{0,8},{8,16},{16,24},{1,9},{9,17},{17,25},{2,10},{10,18},{18,26},{... | collective-permute-start | bytes 27656 | tf_op jit(solution)/shard_map/ppermute | solution.py:16
  66.4 6.3 %collective-permute-start.4 = (f32[1,64,128]{2,1,0:T(8,128)S(1)}, f32[1,64,128]{2,1,0:T(8,128)S(1)}, u32[]{:S(2)}, u32[]{:S(2)}) collective-permute-start(f32[1,64,128]{2,1,0:T(8,128)S(1)} %get-tuple-element.22), channel_id=1, source_target_pairs={{1,0},{2,1},{3,2},{4,3},{5,4},{6,5},{7,6},{9,8},{10,9},{11,10},{12... | collective-permute-start | bytes 98312 | tf_op jit(solution)/shard_map/ppermute | solution.py:17
  70.6 6.7 %collective-permute-start.5 = (f32[1,64,128]{2,1,0:T(8,128)S(1)}, f32[1,64,128]{2,1,0:T(8,128)S(1)}, u32[]{:S(2)}, u32[]{:S(2)}) collective-permute-start(f32[1,64,128]{2,1,0:T(8,128)S(1)} %get-tuple-element.21), channel_id=1, source_target_pairs={{0,1},{1,2},{2,3},{3,4},{4,5},{5,6},{6,7},{8,9},{9,10},{10,11},{11... | collective-permute-start | bytes 98312 | tf_op jit(solution)/shard_map/ppermute | solution.py:16
  77.4 4.5 %collective-permute-start.6 = (f32[18,1,128]{2,1,0:T(1,128)S(1)}, f32[18,1,128]{2,1,0:T(1,128)S(1)}, u32[]{:S(2)}, u32[]{:S(2)}) collective-permute-start(f32[18,1,128]{2,1,0:T(1,128)S(1)} %get-tuple-element.7), channel_id=1, source_target_pairs={{8,0},{16,8},{24,16},{9,1},{17,9},{25,17},{10,2},{18,10},{26,18},{... | collective-permute-start | bytes 27656 | tf_op jit(solution)/shard_map/ppermute | solution.py:17
  79.3 5.0 %collective-permute-start.7 = (f32[18,1,128]{2,1,0:T(1,128)S(1)}, f32[18,1,128]{2,1,0:T(1,128)S(1)}, u32[]{:S(2)}, u32[]{:S(2)}) collective-permute-start(f32[18,1,128]{2,1,0:T(1,128)S(1)} %get-tuple-element.8), channel_id=1, source_target_pairs={{0,8},{8,16},{16,24},{1,9},{9,17},{17,25},{2,10},{10,18},{18,26},{... | collective-permute-start | bytes 27656 | tf_op jit(solution)/shard_map/ppermute | solution.py:16
  131.9 1.4 collective-permute-start.8
  148.5 26.9 %collective-permute-start.13 = (f32[4,32,32]{2,1,0:T(8,128)S(1)}, f32[4,32,32]{2,1,0:T(8,128)}, u32[]{:S(2)}, u32[]{:S(2)}) collective-permute-start(f32[4,32,32]{2,1,0:T(8,128)S(1)} %broadcast_multiply_fusion.2), channel_id=1, source_target_pairs={{0,16},{16,0},{8,24},{24,8},{1,17},{17,1},{9,25},{25,9},{2,18},{18... | collective-permute-start | bytes 49160 | tf_op jit(solution)/shard_map/ppermute | solution.py:29
  148.6 5.9 %collective-permute-start.10 = (f32[1,64,64]{2,1,0:T(8,128)S(1)}, f32[1,64,64]{2,1,0:T(8,128)S(1)}, u32[]{:S(2)}, u32[]{:S(2)}) collective-permute-start(f32[1,64,64]{2,1,0:T(8,128)S(1)} %get-tuple-element.43), channel_id=1, source_target_pairs={{1,0},{2,1},{3,2},{4,3},{5,4},{6,5},{7,6},{9,8},{10,9},{11,10},{12... | collective-permute-start | bytes 49160 | tf_op jit(solution)/shard_map/ppermute | solution.py:17
  150.6 6.7 %collective-permute-start.11 = (f32[1,64,64]{2,1,0:T(8,128)S(1)}, f32[1,64,64]{2,1,0:T(8,128)S(1)}, u32[]{:S(2)}, u32[]{:S(2)}) collective-permute-start(f32[1,64,64]{2,1,0:T(8,128)S(1)} %get-tuple-element.44), channel_id=1, source_target_pairs={{0,1},{1,2},{2,3},{3,4},{4,5},{5,6},{6,7},{8,9},{9,10},{10,11},{11... | collective-permute-start | bytes 49160 | tf_op jit(solution)/shard_map/ppermute | solution.py:16
  173.4 4.3 %collective-permute-start.12 = (f32[4,32,32]{2,1,0:T(8,128)S(1)}, f32[4,32,32]{2,1,0:T(8,128)S(1)}, u32[]{:S(2)}, u32[]{:S(2)}) collective-permute-start(f32[4,32,32]{2,1,0:T(8,128)S(1)} %broadcast_multiply_fusion.3), channel_id=1, source_target_pairs={{0,16},{16,0},{8,24},{24,8},{1,17},{17,1},{9,25},{25,9},{2,18},{18... | collective-permute-start | bytes 49160 | tf_op jit(solution)/shard_map/ppermute | solution.py:29
  178.0 6.2 %collective-permute-start.14 = (f32[1,64,32]{2,1,0:T(8,128)S(1)}, f32[1,64,32]{2,1,0:T(8,128)S(1)}, u32[]{:S(2)}, u32[]{:S(2)}) collective-permute-start(f32[1,64,32]{2,1,0:T(8,128)S(1)} %get-tuple-element.56), channel_id=1, source_target_pairs={{1,0},{2,1},{3,2},{4,3},{5,4},{6,5},{7,6},{9,8},{10,9},{11,10},{12... | collective-permute-start | bytes 24584 | tf_op jit(solution)/shard_map/ppermute | solution.py:17
  180.9 6.7 %collective-permute-start.15 = (f32[1,64,32]{2,1,0:T(8,128)S(1)}, f32[1,64,32]{2,1,0:T(8,128)S(1)}, u32[]{:S(2)}, u32[]{:S(2)}) collective-permute-start(f32[1,64,32]{2,1,0:T(8,128)S(1)} %get-tuple-element.57), channel_id=1, source_target_pairs={{0,1},{1,2},{2,3},{3,4},{4,5},{5,6},{6,7},{8,9},{9,10},{10,11},{11... | collective-permute-start | bytes 24584 | tf_op jit(solution)/shard_map/ppermute | solution.py:16
  209.8 6.0 %collective-permute-start.16 = (f32[1,64,64]{2,1,0:T(8,128)S(1)}, f32[1,64,64]{2,1,0:T(8,128)S(1)}, u32[]{:S(2)}, u32[]{:S(2)}) collective-permute-start(f32[1,64,64]{2,1,0:T(8,128)S(1)} %get-tuple-element.35), channel_id=1, source_target_pairs={{1,0},{2,1},{3,2},{4,3},{5,4},{6,5},{7,6},{9,8},{10,9},{11,10},{12... | collective-permute-start | bytes 49160 | tf_op jit(solution)/shard_map/ppermute | solution.py:17
  211.7 6.7 %collective-permute-start.17 = (f32[1,64,64]{2,1,0:T(8,128)S(1)}, f32[1,64,64]{2,1,0:T(8,128)S(1)}, u32[]{:S(2)}, u32[]{:S(2)}) collective-permute-start(f32[1,64,64]{2,1,0:T(8,128)S(1)} %get-tuple-element.36), channel_id=1, source_target_pairs={{0,1},{1,2},{2,3},{3,4},{4,5},{5,6},{6,7},{8,9},{9,10},{10,11},{11... | collective-permute-start | bytes 49160 | tf_op jit(solution)/shard_map/ppermute | solution.py:16
  256.1 6.1 %collective-permute-start.18 = (f32[1,64,128]{2,1,0:T(8,128)S(1)}, f32[1,64,128]{2,1,0:T(8,128)S(1)}, u32[]{:S(2)}, u32[]{:S(2)}) collective-permute-start(f32[1,64,128]{2,1,0:T(8,128)S(1)} %get-tuple-element.16), channel_id=1, source_target_pairs={{1,0},{2,1},{3,2},{4,3},{5,4},{6,5},{7,6},{9,8},{10,9},{11,10},{12... | collective-permute-start | bytes 98312 | tf_op jit(solution)/shard_map/ppermute | solution.py:17
  259.0 6.7 %collective-permute-start.19 = (f32[1,64,128]{2,1,0:T(8,128)S(1)}, f32[1,64,128]{2,1,0:T(8,128)S(1)}, u32[]{:S(2)}, u32[]{:S(2)}) collective-permute-start(f32[1,64,128]{2,1,0:T(8,128)S(1)} %get-tuple-element.15), channel_id=1, source_target_pairs={{0,1},{1,2},{2,3},{3,4},{4,5},{5,6},{6,7},{8,9},{9,10},{10,11},{11... | collective-permute-start | bytes 98312 | tf_op jit(solution)/shard_map/ppermute | solution.py:16
  265.7 4.6 %collective-permute-start.20 = (f32[18,1,128]{2,1,0:T(1,128)S(1)}, f32[18,1,128]{2,1,0:T(1,128)S(1)}, u32[]{:S(2)}, u32[]{:S(2)}) collective-permute-start(f32[18,1,128]{2,1,0:T(1,128)S(1)} %get-tuple-element.5), channel_id=1, source_target_pairs={{8,0},{16,8},{24,16},{9,1},{17,9},{25,17},{10,2},{18,10},{26,18},{... | collective-permute-start | bytes 27656 | tf_op jit(solution)/shard_map/ppermute | solution.py:17
  267.7 5.4 %collective-permute-start.21 = (f32[18,1,128]{2,1,0:T(1,128)S(1)}, f32[18,1,128]{2,1,0:T(1,128)S(1)}, u32[]{:S(2)}, u32[]{:S(2)}) collective-permute-start(f32[18,1,128]{2,1,0:T(1,128)S(1)} %get-tuple-element.6), channel_id=1, source_target_pairs={{0,8},{8,16},{16,24},{1,9},{9,17},{17,25},{2,10},{10,18},{18,26},{... | collective-permute-start | bytes 27656 | tf_op jit(solution)/shard_map/ppermute | solution.py:16
where the time goes:
time: 276 us; the launch traced here: 274 us
  local copies, waits for them, and re-layouts  151 us (55%)
  starting transfers between devices  50.9 us (18%)
  other arithmetic  45 us (16%)
  waiting for transfers between devices  27.3 us (10%)
    reshape x4, local copies, waits for them, and re-layouts, restrict(): field.reshape(nx // 2, 2, ny // 2, 2, nz // 2, 2).sum(axis=(1, 3, 5)) * 0.5  90.6 us
    reshape x3, local copies, waits for them, and re-layouts, prolong(): return spread.reshape(2 * nx, 2 * ny, 2 * nz)  40.3 us
    reduce_sum x4, other arithmetic, restrict(): field.reshape(nx // 2, 2, ny // 2, 2, nz // 2, 2).sum(axis=(1, 3, 5)) * 0.5  32.5 us
    ppermute x9, starting transfers between devices, padded_2(): before = lax.ppermute(last, axis, up)  25.2 us
    ppermute x9, waiting for transfers between devices, padded_2(): before = lax.ppermute(last, axis, up)  24.5 us
    ppermute x9, starting transfers between devices, padded_2(): after = lax.ppermute(first, axis, down)  23.5 us
    broadcast_in_dim x2, local copies, waits for them, and re-layouts, prolong(): jnp.broadcast_to(field[:, None, :, None, :, None], (nx, 2, ny, 2, nz, 2))  15.3 us
  transfers between devices with their start and end apart: 22, of which 10 were waited for; matrix products, arithmetic and copies ran while one was open for 43% of the time, Pallas kernels for 0%

commit v1 on v0

v1 whole, which is shorter than its diff:
```python
import functools

import jax
import jax.numpy as jnp
from jax import lax
from jax.experimental import pallas as pl
from jax.experimental.pallas import tpu as pltpu
from jax.sharding import PartitionSpec as P

OMEGA = 0.8
WIDE = 2
EDGE = 8
TOP = 16

SIDES = [(dx, dy) for dx in (-1, 0, 1) for dy in (-1, 0, 1) if (dx, dy) != (0, 0)]


def padded_shape(nx, ny, nz):
    return (nx + 2 * WIDE, ny + 2 * TOP, nz)


def depth_pair(field, step):
    axis = field.ndim - 1
    depth = field.shape[axis]
    column = lax.broadcasted_iota(jnp.int32, field.shape, axis)
    ahead = jnp.where(column < depth - step, pltpu.roll(field, depth - step, axis), 0.0)
    behind = jnp.where(column >= step, pltpu.roll(field, step, axis), 0.0)
    return ahead + behind


def depth_sum(field, step):
    axis = field.ndim - 1
    depth = field.shape[axis]
    column = lax.broadcasted_iota(jnp.int32, field.shape, axis)
    ahead = pltpu.roll(field, depth - step, axis)
    behind = pltpu.roll(field, step, axis)
    return field + jnp.where((column // step) % 2 == 0, ahead, behind)


def around(ref, i, first, count, step, cut=None):
    rows = pl.ds(first, count)
    own = ref[i, rows]
    up = ref[i, pl.ds(first - 1, count)]
    down = ref[i, pl.ds(first + 1, count)]
    if cut is not None:
        up = up * cut[0]
        down = down * cut[1]
    total = ref[i - 1, rows] + ref[i + 1, rows] + (up + down)
    return own, total + depth_pair(own, step)


def loop(low, high, body, unroll=2):
    def step(i, carry):
        body(i)
        return carry

    lax.fori_loop(low, high, step, 0, unroll=unroll)


def halo_copies(ref, nx, ny, planes, corners, sems, base):
    copies = []
    blk, agg = lax.axis_index("blk"), lax.axis_index("agg")
    for dx, dy in SIDES:
        if dx != 0 and dy != 0 and not corners:
            continue
        x_from, x_to, x_count = {
            -1: (WIDE, nx + WIDE, planes),
            0: (WIDE, WIDE, nx),
            1: (nx + WIDE - planes, WIDE - planes, planes),
        }[dx]
        y_from, y_to, y_count = {
            -1: (TOP, TOP + ny, EDGE),
            0: (TOP, TOP, ny),
            1: (TOP + ny - EDGE, TOP - EDGE, EDGE),
        }[dy]
        at = base + len(copies)
        copy = pltpu.make_async_remote_copy(
            src_ref=ref.at[pl.ds(x_from, x_count), pl.ds(y_from, y_count)],
            dst_ref=ref.at[pl.ds(x_to, x_count), pl.ds(y_to, y_count)],
            send_sem=sems[0].at[at],
            recv_sem=sems[1].at[at],
            device_id={"blk": blk + dx, "agg": agg + dy},
            device_id_type=pl.DeviceIdType.MESH,
        )
        copies.append(((dx, dy), copy))
    return copies


def kernel(levels, *refs):
    refs = list(refs)
    rhs_ref, coef_ref, out_ref = refs[:3]
    refs = refs[3:]
    take = lambda count: [refs.pop(0) for _ in range(count)]
    vs = take(levels + 1)
    ws = take(levels + 1)
    ps = take(levels + 1)
    bs = take(levels + 1)
    cs = take(levels + 1)
    ts = take(levels)
    us = take(levels)
    sems = take(2)

    nx, ny, nz = rhs_ref.shape
    shapes = [(nx >> k, ny >> k, nz) for k in range(levels + 1)]
    blk, agg = lax.axis_index("blk"), lax.axis_index("agg")
    n_blk, n_agg = lax.axis_size("blk"), lax.axis_size("agg")

    def inside(dx, dy):
        ok = None
        for d, at, size in ((dx, blk, n_blk), (dy, agg, n_agg)):
            if d == 0:
                continue
            this = at > 0 if d < 0 else at < size - 1
            ok = this if ok is None else jnp.logical_and(ok, this)
        return ok

    barrier = pltpu.get_barrier_semaphore()
    for dx, dy in SIDES:

        @pl.when(inside(dx, dy))
        def _():
            pl.semaphore_signal(
                barrier,
                inc=1,
                device_id={"blk": blk + dx, "agg": agg + dy},
                device_id_type=pl.DeviceIdType.MESH,
            )

    @pl.when(blk == 0)
    def _():
        for ref in vs + ws:
            ref[0:WIDE] = jnp.zeros((WIDE,) + ref.shape[1:], jnp.float32)

    @pl.when(blk == n_blk - 1)
    def _():
        for ref in vs + ws:
            high = ref.shape[0]
            ref[high - WIDE : high] = jnp.zeros((WIDE,) + ref.shape[1:], jnp.float32)

    @pl.when(agg == 0)
    def _():
        for ref in vs + ws:
            zero = jnp.zeros((ref.shape[0], EDGE, nz), jnp.float32)
            ref[:, TOP - EDGE : TOP] = zero

    @pl.when(agg == n_agg - 1)
    def _():
        for ref in vs + ws:
            high = ref.shape[1] - TOP
            zero = jnp.zeros((ref.shape[0], EDGE, nz), jnp.float32)
            ref[:, high : high + EDGE] = zero

    own_rows = pl.ds(TOP, ny)

    def guess(i):
        scale = OMEGA / (6.0 + coef_ref[i])
        ws[0][i + WIDE, own_rows] = scale
        vs[0][i + WIDE, own_rows] = scale * rhs_ref[i]

    loop(0, nx, guess)

    count = 1
    for size, at in ((n_blk, blk), (n_agg, agg)):
        near = 1 + (at > 0).astype(jnp.int32) + (at < size - 1).astype(jnp.int32)
        count = count * near
    pl.semaphore_wait(barrier, count - 1)

    pending = []
    used = [0]

    def send(ref, k, planes, corners):
        copies = halo_copies(ref, *shapes[k][:2], planes, corners, sems, used[0])
        used[0] += len(copies)
        for (dx, dy), copy in copies:

            @pl.when(inside(dx, dy))
            def _():
                copy.start()

        pending.extend(copies)
        return copies

    def receive(copies):
        for (dx, dy), copy in copies:

            @pl.when(inside(-dx, -dy))
            def _():
                copy.wait_recv()

    def coarsened(source, k, i):
        rows = shapes[k][1]
        held = ts[k - 1]
        held[i] = source
        pair = held[i, pl.ds(0, rows, stride=2)] + held[i, pl.ds(1, rows, stride=2)]
        return 0.5 * depth_sum(pair, 1 << (k - 1))

    v_moves = [send(vs[0], 0, WIDE, True)]
    w_moves = [send(ws[0], 0, 1, False)]

    for k in range(1, levels + 1):
        above = coef_ref if k == 1 else cs[k - 1]

        def scales(i, k=k, above=above):
            coef = coarsened(above[2 * i] + above[2 * i + 1], k, i)
            cs[k][i] = coef
            ws[k][i + WIDE, pl.ds(TOP, shapes[k][1])] = OMEGA / (6.0 + coef)

        loop(0, shapes[k][0], scales)
        w_moves.append(send(ws[k], k, 1, k > 1))

    receive(v_moves[0])
    receive(w_moves[0])

    def smooth_fine(i):
        own, total = around(vs[0], i, TOP - EDGE, ny + 2 * EDGE, 1)
        ps[0][i, pl.ds(TOP - EDGE, ny + 2 * EDGE)] = (
            1.2 * own + ws[0][i, pl.ds(TOP - EDGE, ny + 2 * EDGE)] * total
        )
        return total[EDGE : EDGE + ny]

    def smooth_own(i):
        total = smooth_fine(i + WIDE)
        bs[0][i] = 0.04 * rhs_ref[i] - OMEGA * total

    smooth_fine(WIDE - 1)
    loop(0, nx, smooth_own)
    smooth_fine(nx + WIDE)

    def fine_residual(i):
        _, total = around(ps[0], i + WIDE, TOP, ny, 1)
        return bs[0][i] + total

    def cuts(k, first, rows):
        span = 1 << k
        low = (agg % span != 0).astype(jnp.float32)
        high = ((agg + 1) % span != 0).astype(jnp.float32)
        row = first + lax.broadcasted_iota(jnp.int32, (rows, nz), 0)
        end = TOP + shapes[k][1]
        up = jnp.where(row == TOP, low, jnp.where(row == end, high, 1.0))
        down = jnp.where(row == TOP - 1, low, jnp.where(row == end - 1, high, 1.0))
        return up, down

    for k in range(1, levels + 1):
        kx, ky, _ = shapes[k]
        if k == 1:
            residual = fine_residual
        else:
            cut = cuts(k - 1, TOP, shapes[k - 1][1])

            def residual(i, k=k, cut=cut):
                _, total = around(
                    vs[k - 1], i + WIDE, TOP, shapes[k - 1][1], 1 << (k - 1), cut
                )
                return 0.2 * bs[k - 1][i] + total

        def descend(i, k=k, residual=residual):
            source = coarsened(residual(2 * i) + residual(2 * i + 1), k, i)
            bs[k][i] = source
            rows = pl.ds(TOP, shapes[k][1])
            vs[k][i + WIDE, rows] = ws[k][i + WIDE, rows] * source

        loop(0, kx, descend)
        v_moves.append(send(vs[k], k, WIDE, True))
        receive(v_moves[k])

    for k in range(1, levels + 1):
        receive(w_moves[k])

    def spread(k, i):
        count = shapes[k + 1][1] + EDGE
        coarse = cs_error[k + 1][i, pl.ds(TOP - EDGE // 2, count)]
        us[k][i, pl.ds(TOP - EDGE, count, stride=2)] = coarse
        us[k][i, pl.ds(TOP - EDGE + 1, count, stride=2)] = coarse
        return us[k][i, pl.ds(TOP - EDGE, 2 * count)]

    cs_error = es = [None] + take(levels)

    for k in range(levels, 0, -1):
        kx, ky, _ = shapes[k]
        rows = pl.ds(TOP - EDGE, ky + 2 * EDGE)
        cut = cuts(k, TOP - EDGE, ky + 2 * EDGE)
        if k == levels:

            def relax(i, k=k, rows=rows, cut=cut, ky=ky):
                own, total = around(vs[k], i, TOP - EDGE, ky + 2 * EDGE, 1 << k, cut)
                es[k][i, rows] = 1.2 * own + ws[k][i, rows] * total
        else:

            def merge(i, k=k, rows=rows):
                extra = spread(k, i)
                for j in range(2):
                    at = 2 * (i - 1) + j
                    ps[k][at, rows] = vs[k][at, rows] + extra

            loop(1, shapes[k + 1][0] + WIDE + 1, merge)

            def relax(i, k=k, rows=rows, cut=cut, ky=ky):
                own, total = around(ps[k], i, TOP - EDGE, ky + 2 * EDGE, 1 << k, cut)
                es[k][i, rows] = 0.2 * own + (vs[k][i, rows] + ws[k][i, rows] * total)

        loop(1, kx + WIDE + 1, relax)

    def merge_fine(i):
        extra = spread(0, i)
        rows = pl.ds(TOP - EDGE, ny + 2 * EDGE)
        for j in range(2):
            at = 2 * (i - 1) + j
            ps[0][at, rows] = ps[0][at, rows] + extra

    loop(1, shapes[1][0] + WIDE + 1, merge_fine)

    def finish(i):
        own, total = around(ps[0], i + WIDE, TOP, ny, 1)
        at = i + WIDE
        out_ref[i] = 0.2 * own + (vs[0][at, own_rows] + ws[0][at, own_rows] * total)

    loop(0, nx, finish)

    for (dx, dy), copy in pending:

        @pl.when(inside(dx, dy))
        def _():
            copy.wait_send()


def shards(right_side, coefficient):
    levels = lax.axis_size("agg").bit_length() - 1
    nx, ny, nz = right_side.shape
    shapes = [(nx >> k, ny >> k, nz) for k in range(levels + 1)]
    vmem = lambda shape: pltpu.VMEM(shape, jnp.float32)
    padded = [vmem(padded_shape(*shape)) for shape in shapes]
    plain = [vmem(shape) for shape in shapes]
    halves = [vmem((shapes[k + 1][0], shapes[k][1], nz)) for k in range(levels)]
    spreads = [
        vmem((shapes[k + 1][0] + 2 * WIDE, shapes[k][1] + 2 * TOP, nz)) for k in range(levels)
    ]
    moves = 16 * (levels + 1)
    sems = [pltpu.SemaphoreType.DMA((moves,))] * 2
    cells = nx * ny * nz
    return pl.pallas_call(
        functools.partial(kernel, levels),
        out_shape=jax.ShapeDtypeStruct(right_side.shape, right_side.dtype),
        in_specs=[pl.BlockSpec(memory_space=pltpu.VMEM)] * 2,
        out_specs=pl.BlockSpec(memory_space=pltpu.VMEM),
        scratch_shapes=padded * 3 + plain * 2 + halves + spreads + sems + padded[1:],
        compiler_params=pltpu.CompilerParams(
            collective_id=0, has_side_effects=True, vmem_limit_bytes=40 * 2**20
        ),
        cost_estimate=pl.CostEstimate(
            flops=60 * cells, bytes_accessed=12 * cells, transcendentals=0
        ),
        name="vcycle",
    )(right_side, coefficient)


def solution(mesh):
    placed = (P("blk", "agg", None), P("blk", "agg", None))
    return jax.shard_map(
        shards, mesh=mesh, in_specs=placed, out_specs=P("blk", "agg", None), check_vma=False
    )
```

time: 276 us -> 26.2 us (0.09)
  the two profiles are of different devices: /device:TPU:28 before, /device:TPU:1 now
where the time goes in v1:
time: 26.2 us; the launch traced here: 26 us
  Pallas kernels  23.1 us (88%)
  local copies, waits for them, and re-layouts  2.88 us (11%)
    pallas_call x1, Pallas kernels, shards(): pl.pallas_call(functools.partial(kernel, levels), out_shape=jax.ShapeDtyp...  23.1 us
    unnamed x5, local copies, waits for them, and re-layouts  2.88 us

profile of v1, /device:TPU:1, one launch (start us, length us, event | category | flops | bytes accessed | tf_op | source)
XLA Modules:
  0.0 26.0 jit_solution(9700501147128254058)
XLA Ops:
  0.0 0.0 copy-start
  0.0 1.0 %copy-done = f32[16,64,128]{2,1,0:T(8,128)S(1)} copy-done((f32[16,64,128]{2,1,0:T(8,128)S(1)}, f32[16,64,128]{2,1,0:T(8,128)}, u32[]{:S(2)}) %copy-start) | copy-done | bytes 524312
  1.0 0.0 copy-start.1
  1.0 1.0 %copy-done.1 = f32[16,64,128]{2,1,0:T(8,128)S(1)} copy-done((f32[16,64,128]{2,1,0:T(8,128)S(1)}, f32[16,64,128]{2,1,0:T(8,128)}, u32[]{:S(2)}) %copy-start.1) | copy-done | bytes 524312
  2.1 23.1 %vcycle.1 = f32[16,64,128]{2,1,0:T(8,128)S(1)} custom-call(f32[16,64,128]{2,1,0:T(8,128)S(1)} %copy-done, f32[16,64,128]{2,1,0:T(8,128)S(1)} %copy-done.1), custom_call_target="tpu_custom_call" | custom-call | flops 7864320 | bytes 1572864 | tf_op jit(solution)/shard_map/vcycle/pallas_call | solution.py:340
  25.2 0.8 %copy.4 = f32[16,64,128]{2,1,0:T(8,128)} copy(f32[16,64,128]{2,1,0:T(8,128)S(1)} %vcycle.1) | data formatting | bytes 1048576
Async XLA Ops:
  0.0 1.0 %copy-start = (f32[16,64,128]{2,1,0:T(8,128)S(1)}, f32[16,64,128]{2,1,0:T(8,128)}, u32[]{:S(2)}) copy-start(f32[16,64,128]{2,1,0:T(8,128)} %refs_0_.1) | copy-start | bytes 1572868
  1.0 1.0 %copy-start.1 = (f32[16,64,128]{2,1,0:T(8,128)S(1)}, f32[16,64,128]{2,1,0:T(8,128)}, u32[]{:S(2)}) copy-start(f32[16,64,128]{2,1,0:T(8,128)} %refs_1_.1) | copy-start | bytes 1572868

commit v2 on v1

--- a/solution.py
+++ b/solution.py
@@ -49,16 +49,33 @@
     return own, total + depth_pair(own, step)
 
 
-def loop(low, high, body, unroll=2):
+UNROLL = 4
+
+
+def loop(low, high, body, unroll=UNROLL):
+    trips = high - low
+    if trips <= unroll:
+        for i in range(low, high):
+            body(i)
+        return
+    while trips % unroll:
+        unroll -= 1
+
     def step(i, carry):
-        body(i)
+        for j in range(unroll):
+            body(low + i * unroll + j)
         return carry
 
-    lax.fori_loop(low, high, step, 0, unroll=unroll)
+    lax.fori_loop(0, trips // unroll, step, 0)
+
+
+X_FACES = [(-1, 0), (1, 0)]
+Y_FACES = [(0, -1), (0, 1)]
+CORNERS = [(-1, -1), (-1, 1), (1, -1), (1, 1)]
 
 
 def halo_copies(ref, nx, ny, planes, corners, sems, base):
-    copies = []
+    copies = {}
     blk, agg = lax.axis_index("blk"), lax.axis_index("agg")
     for dx, dy in SIDES:
         if dx != 0 and dy != 0 and not corners:
@@ -82,28 +99,42 @@
             device_id={"blk": blk + dx, "agg": agg + dy},
             device_id_type=pl.DeviceIdType.MESH,
         )
-        copies.append(((dx, dy), copy))
+        copies[dx, dy] = copy
     return copies
 
 
 def kernel(levels, *refs):
     refs = list(refs)
-    rhs_ref, coef_ref, out_ref = refs[:3]
+    rhs_hbm, coef_hbm, out_hbm = refs[:3]
     refs = refs[3:]
     take = lambda count: [refs.pop(0) for _ in range(count)]
     vs = take(levels + 1)
     ws = take(levels + 1)
-    ps = take(levels + 1)
+    fs = take(levels + 1)
     bs = take(levels + 1)
     cs = take(levels + 1)
     ts = take(levels)
     us = take(levels)
-    sems = take(2)
+    ps, rhs_ref = take(2)
+    coef_ref = cs[0]
+    send_sem, recv_sem, load_sem, store_sem = take(4)
+    out_ref = rhs_ref
 
     nx, ny, nz = rhs_ref.shape
     shapes = [(nx >> k, ny >> k, nz) for k in range(levels + 1)]
     blk, agg = lax.axis_index("blk"), lax.axis_index("agg")
     n_blk, n_agg = lax.axis_size("blk"), lax.axis_size("agg")
+
+    part = nx // 4
+    loads = {}
+    for at, q in enumerate((0, 3, 1, 2)):
+        planes = pl.ds(q * part, part)
+        loads[q] = [
+            pltpu.make_async_copy(hbm.at[planes], ref.at[planes], load_sem.at[2 * at + j])
+            for j, (hbm, ref) in enumerate(((coef_hbm, coef_ref), (rhs_hbm, rhs_ref)))
+        ]
+        for copy in loads[q]:
+            copy.start()
 
     def inside(dx, dy):
         ok = None
@@ -150,6 +181,33 @@
             zero = jnp.zeros((ref.shape[0], EDGE, nz), jnp.float32)
             ref[:, high : high + EDGE] = zero
 
+    used = 0
+    v_moves, w_moves = [], []
+    for k in range(levels + 1):
+        for ref, moves, planes, corners in (
+            (vs[k], v_moves, WIDE, True),
+            (ws[k], w_moves, 1, k > 1),
+        ):
+            copies = halo_copies(
+                ref, *shapes[k][:2], planes, corners, (send_sem, recv_sem), used
+            )
+            moves.append(copies)
+            used += len(copies)
+
+    def send(copies, sides):
+        for dx, dy in sides:
+
+            @pl.when(inside(dx, dy))
+            def _():
+                copies[dx, dy].start()
+
+    def receive(copies, sides):
+        for dx, dy in sides:
+
+            @pl.when(inside(-dx, -dy))
+            def _():
+                copies[dx, dy].wait_recv()
+
     own_rows = pl.ds(TOP, ny)
 
     def guess(i):
@@ -157,35 +215,25 @@
         ws[0][i + WIDE, own_rows] = scale
         vs[0][i + WIDE, own_rows] = scale * rhs_ref[i]
 
-    loop(0, nx, guess)
-
+    def guess_part(q):
+        for copy in loads[q]:
+            copy.wait()
+        loop(q * part, (q + 1) * part, guess)
+
+    guess_part(0)
+    guess_part(3)
     count = 1
     for size, at in ((n_blk, blk), (n_agg, agg)):
         near = 1 + (at > 0).astype(jnp.int32) + (at < size - 1).astype(jnp.int32)
         count = count * near
     pl.semaphore_wait(barrier, count - 1)
-
-    pending = []
-    used = [0]
-
-    def send(ref, k, planes, corners):
-        copies = halo_copies(ref, *shapes[k][:2], planes, corners, sems, used[0])
-        used[0] += len(copies)
-        for (dx, dy), copy in copies:
-
-            @pl.when(inside(dx, dy))
-            def _():
-                copy.start()
-
-        pending.extend(copies)
-        return copies
-
-    def receive(copies):
-        for (dx, dy), copy in copies:
-
-            @pl.when(inside(-dx, -dy))
-            def _():
-                copy.wait_recv()
+    send(v_moves[0], X_FACES)
+    send(w_moves[0], X_FACES)
+    send(v_moves[0], CORNERS)
+    guess_part(1)
+    guess_part(2)
+    send(v_moves[0], Y_FACES)
+    send(w_moves[0], Y_FACES)
 
     def coarsened(source, k, i):
         rows = shapes[k][1]
@@ -194,40 +242,31 @@
         pair = held[i, pl.ds(0, rows, stride=2)] + held[i, pl.ds(1, rows, stride=2)]
         return 0.5 * depth_sum(pair, 1 << (k - 1))
 
-    v_moves = [send(vs[0], 0, WIDE, True)]
-    w_moves = [send(ws[0], 0, 1, False)]
-
     for k in range(1, levels + 1):
-        above = coef_ref if k == 1 else cs[k - 1]
-
-        def scales(i, k=k, above=above):
-            coef = coarsened(above[2 * i] + above[2 * i + 1], k, i)
+
+        def scales(i, k=k):
+            coef = coarsened(cs[k - 1][2 * i] + cs[k - 1][2 * i + 1], k, i)
             cs[k][i] = coef
             ws[k][i + WIDE, pl.ds(TOP, shapes[k][1])] = OMEGA / (6.0 + coef)
 
         loop(0, shapes[k][0], scales)
-        w_moves.append(send(ws[k], k, 1, k > 1))
-
-    receive(v_moves[0])
-    receive(w_moves[0])
+        send(w_moves[k], list(w_moves[k]))
+
+    fine_rows = pl.ds(TOP - EDGE, ny + 2 * EDGE)
 
     def smooth_fine(i):
         own, total = around(vs[0], i, TOP - EDGE, ny + 2 * EDGE, 1)
-        ps[0][i, pl.ds(TOP - EDGE, ny + 2 * EDGE)] = (
-            1.2 * own + ws[0][i, pl.ds(TOP - EDGE, ny + 2 * EDGE)] * total
-        )
+        ps[i, fine_rows] = 1.2 * own + ws[0][i, fine_rows] * total
         return total[EDGE : EDGE + ny]
 
     def smooth_own(i):
         total = smooth_fine(i + WIDE)
         bs[0][i] = 0.04 * rhs_ref[i] - OMEGA * total
 
-    smooth_fine(WIDE - 1)
-    loop(0, nx, smooth_own)
-    smooth_fine(nx + WIDE)
-
     def fine_residual(i):
-        _, total = around(ps[0], i + WIDE, TOP, ny, 1)
+        own, total = around(ps, i + WIDE, TOP, ny, 1)
+        at = i + WIDE
+        fs[0][at, own_rows] = 0.2 * own + (vs[0][at, own_rows] + ws[0][at, own_rows] * total)
         return bs[0][i] + total
 
     def cuts(k, first, rows):
@@ -240,6 +279,26 @@
         down = jnp.where(row == TOP - 1, low, jnp.where(row == end - 1, high, 1.0))
         return up, down
 
+    def relax(k):
+        ky = shapes[k][1]
+        cut = cuts(k, TOP - EDGE, ky + 2 * EDGE)
+        rows = pl.ds(TOP - EDGE, ky + 2 * EDGE)
+
+        def body(i):
+            own, total = around(vs[k], i, TOP - EDGE, ky + 2 * EDGE, 1 << k, cut)
+            result = 1.2 * own + ws[k][i, rows] * total
+            if k == levels:
+                spread(k, i, result)
+            else:
+                fs[k][i, rows] = result
+
+        loop(1, shapes[k][0] + WIDE + 1, body)
+
+    def spread(k, i, error):
+        count = shapes[k][1] + 2 * EDGE
+        us[k - 1][i, pl.ds(0, count, stride=2)] = error
+        us[k - 1][i, pl.ds(1, count, stride=2)] = error
+
     for k in range(1, levels + 1):
         kx, ky, _ = shapes[k]
         if k == 1:
@@ -259,68 +318,79 @@
             rows = pl.ds(TOP, shapes[k][1])
             vs[k][i + WIDE, rows] = ws[k][i + WIDE, rows] * source
 
-        loop(0, kx, descend)
-        v_moves.append(send(vs[k], k, WIDE, True))
-        receive(v_moves[k])
-
-    for k in range(1, levels + 1):
-        receive(w_moves[k])
-
-    def spread(k, i):
-        count = shapes[k + 1][1] + EDGE
-        coarse = cs_error[k + 1][i, pl.ds(TOP - EDGE // 2, count)]
-        us[k][i, pl.ds(TOP - EDGE, count, stride=2)] = coarse
-        us[k][i, pl.ds(TOP - EDGE + 1, count, stride=2)] = coarse
-        return us[k][i, pl.ds(TOP - EDGE, 2 * count)]
-
-    cs_error = es = [None] + take(levels)
-
-    for k in range(levels, 0, -1):
+        receive(v_moves[k - 1], Y_FACES)
+        if k == 1:
+            receive(w_moves[0], Y_FACES)
+            loop(1, nx - 1, smooth_own)
+        loop(1, kx - 1, descend)
+        receive(v_moves[k - 1], X_FACES)
+        if k == 1:
+            receive(v_moves[0], CORNERS)
+            receive(w_moves[0], X_FACES)
+            smooth_fine(WIDE - 1)
+            smooth_own(0)
+            smooth_own(nx - 1)
+            smooth_fine(nx + WIDE)
+        descend(0)
+        descend(kx - 1)
+        send(v_moves[k], X_FACES + Y_FACES + CORNERS)
+        if k > 1:
+            receive(v_moves[k - 1], CORNERS)
+            receive(w_moves[k - 1], list(w_moves[k - 1]))
+            relax(k - 1)
+
+    receive(w_moves[levels], list(w_moves[levels]))
+    receive(v_moves[levels], SIDES)
+    relax(levels)
+
+    for k in range(levels - 1, -1, -1):
         kx, ky, _ = shapes[k]
-        rows = pl.ds(TOP - EDGE, ky + 2 * EDGE)
-        cut = cuts(k, TOP - EDGE, ky + 2 * EDGE)
-        if k == levels:
-
-            def relax(i, k=k, rows=rows, cut=cut, ky=ky):
-                own, total = around(vs[k], i, TOP - EDGE, ky + 2 * EDGE, 1 << k, cut)
-                es[k][i, rows] = 1.2 * own + ws[k][i, rows] * total
+        over = EDGE if k else 0
+        count = ky + 2 * over
+        rows = pl.ds(TOP - over, count)
+        cut = cuts(k, TOP - over, count) if k else None
+
+        def correct(i, k=k, count=count, rows=rows, cut=cut, over=over):
+            coarse = us[k]
+            own = coarse[i, rows]
+            up = coarse[i, pl.ds(TOP - over - 1, count)]
+            down = coarse[i, pl.ds(TOP - over + 1, count)]
+            if cut is not None:
+                up = up * cut[0]
+                down = down * cut[1]
+            inner = own + (up + down) + depth_pair(own, 1 << k)
+            for j in range(2):
+                at = 2 * (i - 1) + j
+                total = inner + coarse[i - 1 + 2 * j, rows]
+                result = fs[k][at, rows] + (0.2 * own + ws[k][at, rows] * total)
+                if k == 0:
+                    out_ref[at - WIDE] = result
+                else:
+                    spread(k, at, result)
+
+        if k == 0:
+            stores = []
+            for q in range(4):
+                loop(WIDE + q * part // 2, WIDE + (q + 1) * part // 2, correct)
+                planes = pl.ds(q * part, part)
+                stores.append(
+                    pltpu.make_async_copy(
+                        out_ref.at[planes], out_hbm.at[planes], store_sem.at[q]
+                    )
+                )
+                stores[q].start()
         else:
-
-            def merge(i, k=k, rows=rows):
-                extra = spread(k, i)
-                for j in range(2):
-                    at = 2 * (i - 1) + j
-                    ps[k][at, rows] = vs[k][at, rows] + extra
-
-            loop(1, shapes[k + 1][0] + WIDE + 1, merge)
-
-            def relax(i, k=k, rows=rows, cut=cut, ky=ky):
-                own, total = around(ps[k], i, TOP - EDGE, ky + 2 * EDGE, 1 << k, cut)
-                es[k][i, rows] = 0.2 * own + (vs[k][i, rows] + ws[k][i, rows] * total)
-
-        loop(1, kx + WIDE + 1, relax)
-
-    def merge_fine(i):
-        extra = spread(0, i)
-        rows = pl.ds(TOP - EDGE, ny + 2 * EDGE)
-        for j in range(2):
-            at = 2 * (i - 1) + j
-            ps[0][at, rows] = ps[0][at, rows] + extra
-
-    loop(1, shapes[1][0] + WIDE + 1, merge_fine)
-
-    def finish(i):
-        own, total = around(ps[0], i + WIDE, TOP, ny, 1)
-        at = i + WIDE
-        out_ref[i] = 0.2 * own + (vs[0][at, own_rows] + ws[0][at, own_rows] * total)
-
-    loop(0, nx, finish)
-
-    for (dx, dy), copy in pending:
-
-        @pl.when(inside(dx, dy))
-        def _():
-            copy.wait_send()
+            loop(1, kx // 2 + WIDE + 1, correct)
+
+    for copy in stores:
+        copy.wait()
+
+    for copies in v_moves + w_moves:
+        for (dx, dy), copy in copies.items():
+
+            @pl.when(inside(dx, dy))
+            def _():
+                copy.wait_send()
 
 
 def shards(right_side, coefficient):
@@ -335,16 +405,16 @@
         vmem((shapes[k + 1][0] + 2 * WIDE, shapes[k][1] + 2 * TOP, nz)) for k in range(levels)
     ]
     moves = 16 * (levels + 1)
-    sems = [pltpu.SemaphoreType.DMA((moves,))] * 2
+    sems = [pltpu.SemaphoreType.DMA((moves,))] * 2 + [pltpu.SemaphoreType.DMA((8,)), pltpu.SemaphoreType.DMA((4,))]
     cells = nx * ny * nz
     return pl.pallas_call(
         functools.partial(kernel, levels),
         out_shape=jax.ShapeDtypeStruct(right_side.shape, right_side.dtype),
-        in_specs=[pl.BlockSpec(memory_space=pltpu.VMEM)] * 2,
-        out_specs=pl.BlockSpec(memory_space=pltpu.VMEM),
-        scratch_shapes=padded * 3 + plain * 2 + halves + spreads + sems + padded[1:],
+        in_specs=[pl.BlockSpec(memory_space=pltpu.HBM)] * 2,
+        out_specs=pl.BlockSpec(memory_space=pltpu.HBM),
+        scratch_shapes=padded * 3 + plain * 2 + halves + spreads + [padded[0], plain[0]] + sems,
         compiler_params=pltpu.CompilerParams(
-            collective_id=0, has_side_effects=True, vmem_limit_bytes=40 * 2**20
+            collective_id=0, has_side_effects=True, vmem_limit_bytes=60 * 2**20
         ),
         cost_estimate=pl.CostEstimate(
             flops=60 * cells, bytes_accessed=12 * cells, transcendentals=0

time: 26.2 us -> 23.4 us (0.89)
  Pallas kernels: 23.1 us -> 21.3 us
  local copies, waits for them, and re-layouts: 2.88 us -> 1.89 us
    pallas_call x1, Pallas kernels: 23.1 us -> 21.3 us  [shards(): pl.pallas_call(functools.partial(kernel, levels), out_shape=jax.ShapeDtyp...]
    unnamed x5 -> x1, local copies, waits for them, and re-layouts: 2.88 us -> 1.89 us
where the time goes in v2:
time: 23.4 us; the launch traced here: 23.2 us
  Pallas kernels  21.3 us (91%)
  local copies, waits for them, and re-layouts  1.89 us (8%)
    pallas_call x1, Pallas kernels, shards(): pl.pallas_call(functools.partial(kernel, levels), out_shape=jax.ShapeDtyp...  21.3 us
    unnamed x1, local copies, waits for them, and re-layouts  1.89 us

profile of v2, /device:TPU:1, one launch (start us, length us, event | category | flops | bytes accessed | tf_op | source)
XLA Modules:
  0.0 23.2 jit_solution(1451994800674597928)
XLA Ops:
  0.0 21.3 %vcycle.1 = f32[16,64,128]{2,1,0:T(8,128)} custom-call(f32[16,64,128]{2,1,0:T(8,128)} %refs_0_.1, f32[16,64,128]{2,1,0:T(8,128)} %refs_1_.1), custom_call_target="tpu_custom_call" | custom-call | flops 7864320 | bytes 1572864 | tf_op jit(solution)/shard_map/vcycle/pallas_call | solution.py:410
  21.3 1.9 %copy.4 = f32[16,64,128]{2,1,0:T(8,128)} copy(f32[16,64,128]{2,1,0:T(8,128)} %vcycle.1) | data formatting | bytes 1048576

commit v3 on v2

--- a/solution.py
+++ b/solution.py
@@ -74,12 +74,15 @@
 CORNERS = [(-1, -1), (-1, 1), (1, -1), (1, 1)]
 
 
-def halo_copies(ref, nx, ny, planes, corners, sems, base):
+def halo_copies(ref, nx, ny, wide, corners, sems, base):
     copies = {}
     blk, agg = lax.axis_index("blk"), lax.axis_index("agg")
     for dx, dy in SIDES:
-        if dx != 0 and dy != 0 and not corners:
-            continue
+        planes = wide
+        if dx != 0 and dy != 0:
+            if not corners:
+                continue
+            planes = corners
         x_from, x_to, x_count = {
             -1: (WIDE, nx + WIDE, planes),
             0: (WIDE, WIDE, nx),
@@ -105,7 +108,7 @@
 
 def kernel(levels, *refs):
     refs = list(refs)
-    rhs_hbm, coef_hbm, out_hbm = refs[:3]
+    rhs_hbm, coef_hbm, out_ref = refs[:3]
     refs = refs[3:]
     take = lambda count: [refs.pop(0) for _ in range(count)]
     vs = take(levels + 1)
@@ -117,8 +120,7 @@
     us = take(levels)
     ps, rhs_ref = take(2)
     coef_ref = cs[0]
-    send_sem, recv_sem, load_sem, store_sem = take(4)
-    out_ref = rhs_ref
+    send_sem, recv_sem, load_sem = take(3)
 
     nx, ny, nz = rhs_ref.shape
     shapes = [(nx >> k, ny >> k, nz) for k in range(levels + 1)]
@@ -185,8 +187,8 @@
     v_moves, w_moves = [], []
     for k in range(levels + 1):
         for ref, moves, planes, corners in (
-            (vs[k], v_moves, WIDE, True),
-            (ws[k], w_moves, 1, k > 1),
+            (vs[k], v_moves, WIDE, WIDE if k > 1 else 1),
+            (ws[k], w_moves, 1, 1 if k > 1 else 0),
         ):
             copies = halo_copies(
                 ref, *shapes[k][:2], planes, corners, (send_sem, recv_sem), used
@@ -369,21 +371,9 @@
                     spread(k, at, result)
 
         if k == 0:
-            stores = []
-            for q in range(4):
-                loop(WIDE + q * part // 2, WIDE + (q + 1) * part // 2, correct)
-                planes = pl.ds(q * part, part)
-                stores.append(
-                    pltpu.make_async_copy(
-                        out_ref.at[planes], out_hbm.at[planes], store_sem.at[q]
-                    )
-                )
-                stores[q].start()
+            loop(WIDE, kx // 2 + WIDE, correct)
         else:
             loop(1, kx // 2 + WIDE + 1, correct)
-
-    for copy in stores:
-        copy.wait()
 
     for copies in v_moves + w_moves:
         for (dx, dy), copy in copies.items():
@@ -405,16 +395,16 @@
         vmem((shapes[k + 1][0] + 2 * WIDE, shapes[k][1] + 2 * TOP, nz)) for k in range(levels)
     ]
     moves = 16 * (levels + 1)
-    sems = [pltpu.SemaphoreType.DMA((moves,))] * 2 + [pltpu.SemaphoreType.DMA((8,)), pltpu.SemaphoreType.DMA((4,))]
+    sems = [pltpu.SemaphoreType.DMA((moves,))] * 2 + [pltpu.SemaphoreType.DMA((8,))]
     cells = nx * ny * nz
     return pl.pallas_call(
         functools.partial(kernel, levels),
-        out_shape=jax.ShapeDtypeStruct(right_side.shape, right_side.dtype),
+        out_shape=pltpu.VMEM(right_side.shape, right_side.dtype),
         in_specs=[pl.BlockSpec(memory_space=pltpu.HBM)] * 2,
-        out_specs=pl.BlockSpec(memory_space=pltpu.HBM),
+        out_specs=pl.BlockSpec(memory_space=pltpu.VMEM),
         scratch_shapes=padded * 3 + plain * 2 + halves + spreads + [padded[0], plain[0]] + sems,
         compiler_params=pltpu.CompilerParams(
-            collective_id=0, has_side_effects=True, vmem_limit_bytes=60 * 2**20
+            collective_id=0, has_side_effects=True, vmem_limit_bytes=58 * 2**20
         ),
         cost_estimate=pl.CostEstimate(
             flops=60 * cells, bytes_accessed=12 * cells, transcendentals=0

time: 23.4 us -> 21.3 us (0.910)
  local copies, waits for them, and re-layouts: 1.89 us -> 0.8 us
  Pallas kernels: 21.3 us -> 20.4 us
    unnamed x1, local copies, waits for them, and re-layouts: 1.89 us -> 0.8 us
    pallas_call x1, Pallas kernels: 21.3 us -> 20.4 us  [shards(): pl.pallas_call(functools.partial(kernel, levels), out_shape=pltpu.VMEM(ri...]
where the time goes in v3:
time: 21.3 us; the launch traced here: 21.2 us
  Pallas kernels  20.4 us (96%)
  local copies, waits for them, and re-layouts  0.8 us (4%)
    pallas_call x1, Pallas kernels, shards(): pl.pallas_call(functools.partial(kernel, levels), out_shape=pltpu.VMEM(ri...  20.4 us
    unnamed x1, local copies, waits for them, and re-layouts  0.8 us

profile of v3, /device:TPU:1, one launch (start us, length us, event | category | flops | bytes accessed | tf_op | source)
XLA Modules:
  0.0 21.2 jit_solution(6135257863307927779)
XLA Ops:
  0.0 20.4 %vcycle.1 = f32[16,64,128]{2,1,0:T(8,128)S(1)} custom-call(f32[16,64,128]{2,1,0:T(8,128)} %refs_0_.1, f32[16,64,128]{2,1,0:T(8,128)} %refs_1_.1), custom_call_target="tpu_custom_call" | custom-call | flops 7864320 | bytes 1572864 | tf_op jit(solution)/shard_map/vcycle/pallas_call | solution.py:400
  20.4 0.8 %copy.4 = f32[16,64,128]{2,1,0:T(8,128)} copy(f32[16,64,128]{2,1,0:T(8,128)S(1)} %vcycle.1) | data formatting | bytes 1048576

commit v4 on v3

--- a/solution.py
+++ b/solution.py
@@ -49,7 +49,7 @@
     return own, total + depth_pair(own, step)
 
 
-UNROLL = 4
+UNROLL = 8
 
 
 def loop(low, high, body, unroll=UNROLL):

time: 21.3 us -> 21 us (0.986)
  Pallas kernels: 20.4 us -> 20.1 us
    pallas_call x1, Pallas kernels: 20.4 us -> 20.1 us  [shards(): pl.pallas_call(functools.partial(kernel, levels), out_shape=pltpu.VMEM(ri...]
where the time goes in v4:
time: 21 us; the launch traced here: 20.9 us
  Pallas kernels  20.1 us (96%)
  local copies, waits for them, and re-layouts  0.8 us (4%)
    pallas_call x1, Pallas kernels, shards(): pl.pallas_call(functools.partial(kernel, levels), out_shape=pltpu.VMEM(ri...  20.1 us
    unnamed x1, local copies, waits for them, and re-layouts  0.8 us

profile of v4, /device:TPU:1, one launch (start us, length us, event | category | flops | bytes accessed | tf_op | source)
XLA Modules:
  0.0 20.9 jit_solution(16168662674641856405)
XLA Ops:
  0.0 20.1 %vcycle.1 = f32[16,64,128]{2,1,0:T(8,128)S(1)} custom-call(f32[16,64,128]{2,1,0:T(8,128)} %refs_0_.1, f32[16,64,128]{2,1,0:T(8,128)} %refs_1_.1), custom_call_target="tpu_custom_call" | custom-call | flops 7864320 | bytes 1572864 | tf_op jit(solution)/shard_map/vcycle/pallas_call | solution.py:400
  20.1 0.8 %copy.4 = f32[16,64,128]{2,1,0:T(8,128)} copy(f32[16,64,128]{2,1,0:T(8,128)S(1)} %vcycle.1) | data formatting | bytes 1048576

commit v5 on v4

--- a/solution.py
+++ b/solution.py
@@ -74,7 +74,7 @@
 CORNERS = [(-1, -1), (-1, 1), (1, -1), (1, 1)]
 
 
-def halo_copies(ref, nx, ny, wide, corners, sems, base):
+def halo_copies(ref, nx, ny, wide, corners, sems, base, packed):
     copies = {}
     blk, agg = lax.axis_index("blk"), lax.axis_index("agg")
     for dx, dy in SIDES:
@@ -94,9 +94,13 @@
             1: (TOP + ny - EDGE, TOP - EDGE, EDGE),
         }[dy]
         at = base + len(copies)
+        source = ref.at[pl.ds(x_from, x_count), pl.ds(y_from, y_count)]
+        target = ref.at[pl.ds(x_to, x_count), pl.ds(y_to, y_count)]
+        if packed is not None and dy == 0:
+            source, target = (packed.at[0], packed.at[3]) if dx < 0 else (packed.at[1], packed.at[2])
         copy = pltpu.make_async_remote_copy(
-            src_ref=ref.at[pl.ds(x_from, x_count), pl.ds(y_from, y_count)],
-            dst_ref=ref.at[pl.ds(x_to, x_count), pl.ds(y_to, y_count)],
+            src_ref=source,
+            dst_ref=target,
             send_sem=sems[0].at[at],
             recv_sem=sems[1].at[at],
             device_id={"blk": blk + dx, "agg": agg + dy},
@@ -119,6 +123,7 @@
     ts = take(levels)
     us = take(levels)
     ps, rhs_ref = take(2)
+    faces = [None] + take(levels)
     coef_ref = cs[0]
     send_sem, recv_sem, load_sem = take(3)
 
@@ -186,12 +191,12 @@
     used = 0
     v_moves, w_moves = [], []
     for k in range(levels + 1):
-        for ref, moves, planes, corners in (
-            (vs[k], v_moves, WIDE, WIDE if k > 1 else 1),
-            (ws[k], w_moves, 1, 1 if k > 1 else 0),
+        for ref, moves, planes, corners, packed in (
+            (vs[k], v_moves, WIDE, WIDE if k > 1 else 1, faces[k]),
+            (ws[k], w_moves, 1, 1 if k > 1 else 0, None),
         ):
             copies = halo_copies(
-                ref, *shapes[k][:2], planes, corners, (send_sem, recv_sem), used
+                ref, *shapes[k][:2], planes, corners, (send_sem, recv_sem), used, packed
             )
             moves.append(copies)
             used += len(copies)
@@ -209,6 +214,27 @@
             @pl.when(inside(-dx, -dy))
             def _():
                 copies[dx, dy].wait_recv()
+
+    def first_half(k):
+        column = lax.broadcasted_iota(jnp.int32, (shapes[k][1], nz), 1)
+        return (column >> (k - 1)) % 2 == 0
+
+    def pack_faces(k):
+        rows = pl.ds(TOP, shapes[k][1])
+        for slot, plane in ((0, WIDE), (1, shapes[k][0])):
+            faces[k][slot] = jnp.where(first_half(k), vs[k][plane, rows], vs[k][plane + 1, rows])
+
+    def receive_faces(k):
+        rows, half = pl.ds(TOP, shapes[k][1]), 1 << (k - 1)
+        for dx, slot, plane in ((1, 2, 0), (-1, 3, shapes[k][0] + WIDE)):
+
+            @pl.when(inside(-dx, 0))
+            def _():
+                v_moves[k][dx, 0].wait_recv()
+                both = faces[k][slot]
+                low = first_half(k)
+                vs[k][plane, rows] = jnp.where(low, both, pltpu.roll(both, half, 1))
+                vs[k][plane + 1, rows] = jnp.where(low, pltpu.roll(both, nz - half, 1), both)
 
     own_rows = pl.ds(TOP, ny)
 
@@ -252,7 +278,6 @@
             ws[k][i + WIDE, pl.ds(TOP, shapes[k][1])] = OMEGA / (6.0 + coef)
 
         loop(0, shapes[k][0], scales)
-        send(w_moves[k], list(w_moves[k]))
 
     fine_rows = pl.ds(TOP - EDGE, ny + 2 * EDGE)
 
@@ -325,9 +350,12 @@
             receive(w_moves[0], Y_FACES)
             loop(1, nx - 1, smooth_own)
         loop(1, kx - 1, descend)
-        receive(v_moves[k - 1], X_FACES)
-        if k == 1:
-            receive(v_moves[0], CORNERS)
+        if k > 1:
+            receive_faces(k - 1)
+        else:
+            for moves in w_moves[1:]:
+                send(moves, list(moves))
+            receive(v_moves[0], X_FACES + CORNERS)
             receive(w_moves[0], X_FACES)
             smooth_fine(WIDE - 1)
             smooth_own(0)
@@ -335,6 +363,7 @@
             smooth_fine(nx + WIDE)
         descend(0)
         descend(kx - 1)
+        pack_faces(k)
         send(v_moves[k], X_FACES + Y_FACES + CORNERS)
         if k > 1:
             receive(v_moves[k - 1], CORNERS)
@@ -342,7 +371,8 @@
             relax(k - 1)
 
     receive(w_moves[levels], list(w_moves[levels]))
-    receive(v_moves[levels], SIDES)
+    receive(v_moves[levels], Y_FACES + CORNERS)
+    receive_faces(levels)
     relax(levels)
 
     for k in range(levels - 1, -1, -1):
@@ -394,6 +424,7 @@
     spreads = [
         vmem((shapes[k + 1][0] + 2 * WIDE, shapes[k][1] + 2 * TOP, nz)) for k in range(levels)
     ]
+    faces = [vmem((4,) + shape[1:]) for shape in shapes[1:]]
     moves = 16 * (levels + 1)
     sems = [pltpu.SemaphoreType.DMA((moves,))] * 2 + [pltpu.SemaphoreType.DMA((8,))]
     cells = nx * ny * nz
@@ -402,7 +433,7 @@
         out_shape=pltpu.VMEM(right_side.shape, right_side.dtype),
         in_specs=[pl.BlockSpec(memory_space=pltpu.HBM)] * 2,
         out_specs=pl.BlockSpec(memory_space=pltpu.VMEM),
-        scratch_shapes=padded * 3 + plain * 2 + halves + spreads + [padded[0], plain[0]] + sems,
+        scratch_shapes=padded * 3 + plain * 2 + halves + spreads + [padded[0], plain[0]] + faces + sems,
         compiler_params=pltpu.CompilerParams(
             collective_id=0, has_side_effects=True, vmem_limit_bytes=58 * 2**20
         ),

time: 21 us -> 20.5 us (0.976)
  Pallas kernels: 20.1 us -> 19.5 us
    pallas_call x1, Pallas kernels: 20.1 us -> 19.5 us  [shards(): pl.pallas_call(functools.partial(kernel, levels), out_shape=pltpu.VMEM(ri...]
where the time goes in v5:
time: 20.5 us; the launch traced here: 20.4 us
  Pallas kernels  19.5 us (95%)
  local copies, waits for them, and re-layouts  0.8 us (4%)
    pallas_call x1, Pallas kernels, shards(): pl.pallas_call(functools.partial(kernel, levels), out_shape=pltpu.VMEM(ri...  19.5 us
    unnamed x1, local copies, waits for them, and re-layouts  0.8 us

profile of v5, /device:TPU:1, one launch (start us, length us, event | category | flops | bytes accessed | tf_op | source)
XLA Modules:
  0.0 20.4 jit_solution(12390044398055974420)
XLA Ops:
  0.0 19.5 %vcycle.1 = f32[16,64,128]{2,1,0:T(8,128)S(1)} custom-call(f32[16,64,128]{2,1,0:T(8,128)} %refs_0_.1, f32[16,64,128]{2,1,0:T(8,128)} %refs_1_.1), custom_call_target="tpu_custom_call" | custom-call | flops 7864320 | bytes 1572864 | tf_op jit(solution)/shard_map/vcycle/pallas_call | solution.py:431
  19.6 0.8 %copy.4 = f32[16,64,128]{2,1,0:T(8,128)} copy(f32[16,64,128]{2,1,0:T(8,128)S(1)} %vcycle.1) | data formatting | bytes 1048576

commit v6 on v5

--- a/solution.py
+++ b/solution.py
@@ -74,10 +74,12 @@
 CORNERS = [(-1, -1), (-1, 1), (1, -1), (1, 1)]
 
 
-def halo_copies(ref, nx, ny, wide, corners, sems, base, packed):
+def halo_copies(ref, nx, ny, wide, corners, sems, base, packed, tiles):
     copies = {}
     blk, agg = lax.axis_index("blk"), lax.axis_index("agg")
     for dx, dy in SIDES:
+        if corners is None and dy != 0:
+            continue
         planes = wide
         if dx != 0 and dy != 0:
             if not corners:
@@ -98,6 +100,8 @@
         target = ref.at[pl.ds(x_to, x_count), pl.ds(y_to, y_count)]
         if packed is not None and dy == 0:
             source, target = (packed.at[0], packed.at[3]) if dx < 0 else (packed.at[1], packed.at[2])
+        if tiles is not None and dx == 0:
+            source = tiles.at[0 if dy < 0 else 1]
         copy = pltpu.make_async_remote_copy(
             src_ref=source,
             dst_ref=target,
@@ -124,6 +128,7 @@
     us = take(levels)
     ps, rhs_ref = take(2)
     faces = [None] + take(levels)
+    tiles = take(1)[0]
     coef_ref = cs[0]
     send_sem, recv_sem, load_sem = take(3)
 
@@ -191,15 +196,35 @@
     used = 0
     v_moves, w_moves = [], []
     for k in range(levels + 1):
-        for ref, moves, planes, corners, packed in (
-            (vs[k], v_moves, WIDE, WIDE if k > 1 else 1, faces[k]),
-            (ws[k], w_moves, 1, 1 if k > 1 else 0, None),
+        for ref, moves, planes, corners, packed, edges in (
+            (vs[k], v_moves, WIDE, WIDE if k > 1 else 1, faces[k], tiles if k == 0 else None),
+            (ws[k], w_moves, 1, (None, 0, 1)[min(k, 2)], None, None),
         ):
             copies = halo_copies(
-                ref, *shapes[k][:2], planes, corners, (send_sem, recv_sem), used, packed
+                ref, *shapes[k][:2], planes, corners, (send_sem, recv_sem), used, packed, edges
             )
             moves.append(copies)
             used += len(copies)
+
+    def pack_tiles(i):
+        row = lax.broadcasted_iota(jnp.int32, (EDGE, nz), 0)
+        for slot, low, kept in ((0, TOP, row < WIDE), (1, TOP + ny - EDGE, row >= EDGE - WIDE)):
+            rows = pl.ds(low, EDGE)
+            scale = pltpu.roll(ws[0][i + WIDE, rows], EDGE // 2, 0)
+            tiles[slot, i] = jnp.where(kept, vs[0][i + WIDE, rows], scale)
+
+    def receive_tiles():
+        for dy, low in ((-1, TOP + ny), (1, TOP - EDGE)):
+
+            @pl.when(inside(0, -dy))
+            def _():
+                v_moves[0][0, dy].wait_recv()
+                rows = pl.ds(low, EDGE)
+
+                def unpack(i):
+                    ws[0][i + WIDE, rows] = pltpu.roll(vs[0][i + WIDE, rows], EDGE // 2, 0)
+
+                loop(0, nx, unpack)
 
     def send(copies, sides):
         for dx, dy in sides:
@@ -260,8 +285,8 @@
     send(v_moves[0], CORNERS)
     guess_part(1)
     guess_part(2)
+    loop(0, nx, pack_tiles)
     send(v_moves[0], Y_FACES)
-    send(w_moves[0], Y_FACES)
 
     def coarsened(source, k, i):
         rows = shapes[k][1]
@@ -345,9 +370,10 @@
             rows = pl.ds(TOP, shapes[k][1])
             vs[k][i + WIDE, rows] = ws[k][i + WIDE, rows] * source
 
-        receive(v_moves[k - 1], Y_FACES)
-        if k == 1:
-            receive(w_moves[0], Y_FACES)
+        if k > 1:
+            receive(v_moves[k - 1], Y_FACES)
+        else:
+            receive_tiles()
             loop(1, nx - 1, smooth_own)
         loop(1, kx - 1, descend)
         if k > 1:
@@ -370,6 +396,15 @@
             receive(w_moves[k - 1], list(w_moves[k - 1]))
             relax(k - 1)
 
+    def drain(moves):
+        for copies in moves:
+            for (dx, dy), copy in copies.items():
+
+                @pl.when(inside(dx, dy))
+                def _():
+                    copy.wait_send()
+
+    drain(v_moves[:levels] + w_moves)
     receive(w_moves[levels], list(w_moves[levels]))
     receive(v_moves[levels], Y_FACES + CORNERS)
     receive_faces(levels)
@@ -405,12 +440,7 @@
         else:
             loop(1, kx // 2 + WIDE + 1, correct)
 
-    for copies in v_moves + w_moves:
-        for (dx, dy), copy in copies.items():
-
-            @pl.when(inside(dx, dy))
-            def _():
-                copy.wait_send()
+    drain(v_moves[levels:])
 
 
 def shards(right_side, coefficient):
@@ -425,6 +455,7 @@
         vmem((shapes[k + 1][0] + 2 * WIDE, shapes[k][1] + 2 * TOP, nz)) for k in range(levels)
     ]
     faces = [vmem((4,) + shape[1:]) for shape in shapes[1:]]
+    tiles = vmem((2, nx, EDGE, nz))
     moves = 16 * (levels + 1)
     sems = [pltpu.SemaphoreType.DMA((moves,))] * 2 + [pltpu.SemaphoreType.DMA((8,))]
     cells = nx * ny * nz
@@ -433,7 +464,7 @@
         out_shape=pltpu.VMEM(right_side.shape, right_side.dtype),
         in_specs=[pl.BlockSpec(memory_space=pltpu.HBM)] * 2,
         out_specs=pl.BlockSpec(memory_space=pltpu.VMEM),
-        scratch_shapes=padded * 3 + plain * 2 + halves + spreads + [padded[0], plain[0]] + faces + sems,
+        scratch_shapes=padded * 3 + plain * 2 + halves + spreads + [padded[0], plain[0]] + faces + [tiles] + sems,
         compiler_params=pltpu.CompilerParams(
             collective_id=0, has_side_effects=True, vmem_limit_bytes=58 * 2**20
         ),

time: 20.5 us -> 20.8 us (1.015)
  Pallas kernels: 19.5 us -> 19.9 us
    pallas_call x1, Pallas kernels: 19.5 us -> 19.9 us  [shards(): pl.pallas_call(functools.partial(kernel, levels), out_shape=pltpu.VMEM(ri...]
where the time goes in v6:
time: 20.8 us; the launch traced here: 20.7 us
  Pallas kernels  19.9 us (96%)
  local copies, waits for them, and re-layouts  0.8 us (4%)
    pallas_call x1, Pallas kernels, shards(): pl.pallas_call(functools.partial(kernel, levels), out_shape=pltpu.VMEM(ri...  19.9 us
    unnamed x1, local copies, waits for them, and re-layouts  0.8 us

profile of v6, /device:TPU:1, one launch (start us, length us, event | category | flops | bytes accessed | tf_op | source)
XLA Modules:
  0.0 20.7 jit_solution(15109830480123588931)
XLA Ops:
  0.0 19.9 %vcycle.1 = f32[16,64,128]{2,1,0:T(8,128)S(1)} custom-call(f32[16,64,128]{2,1,0:T(8,128)} %refs_0_.1, f32[16,64,128]{2,1,0:T(8,128)} %refs_1_.1), custom_call_target="tpu_custom_call" | custom-call | flops 7864320 | bytes 1572864 | tf_op jit(solution)/shard_map/vcycle/pallas_call | solution.py:462
  19.9 0.8 %copy.4 = f32[16,64,128]{2,1,0:T(8,128)} copy(f32[16,64,128]{2,1,0:T(8,128)S(1)} %vcycle.1) | data formatting | bytes 1048576
